TPU v7x, 32 devices: a whole 2x2x4 slice. The times are simulated.
32 devices in a mesh: grp: 2 (over x), feat: 16 (over z, y, core).
Axes of the slice: x: 2, y: 2, z: 4, core: 2. Of those that a mesh axis runs over, the one named last changes fastest.
Arguments:
- inputs: bfloat16 [5120, 4096], P('feat', 'grp'), parts along dimension 1, may hold values from -6 to 6
- pattern: int32 [4, 16], P(None, 'feat'), may hold values 0 or 1
- rank_mask: int32 [128], replicated, may hold values 0 or 1
- up_diag: bfloat16 [20480, 320], P('feat'), may hold values from -0.15625 to 0.15625
- up_cross: bfloat16 [4, 20480, 320], P(None, 'feat'), may hold values from -0.15625 to 0.15625
- up_left: bfloat16 [20480, 128], P('feat'), may hold values from -0.5 to 0.5
- up_right: bfloat16 [5120, 128], P('feat'), may hold values from -0.078125 to 0.078125
- down_diag: bfloat16 [5120, 1280], P('feat'), may hold values from -0.078125 to 0.078125
- down_cross: bfloat16 [4, 5120, 1280], P(None, 'feat'), may hold values from -0.078125 to 0.078125
- down_left: bfloat16 [5120, 128], P('feat'), may hold values from -0.5 to 0.5
- down_right: bfloat16 [20480, 128], P('feat'), may hold values from -0.0390625 to 0.0390625
- cotangent: bfloat16 [5120, 4096], P('feat', 'grp'), parts along dimension 1, may hold values from -6 to 6
Outputs:
- output: bfloat16 [5120, 4096], P('feat', 'grp'), parts along dimension 1
- input_grad: bfloat16 [5120, 4096], P('feat', 'grp'), parts along dimension 1
- grad_up_diag: float32 [20480, 640], P('feat', 'grp'), parts along dimension 1
- grad_up_cross: float32 [4, 20480, 640], P(None, 'feat', 'grp'), parts along dimension 2
- grad_up_left: float32 [20480, 256], P('feat', 'grp'), parts along dimension 1
- grad_up_right: float32 [5120, 256], P('feat', 'grp'), parts along dimension 1
- grad_down_diag: float32 [5120, 2560], P('feat', 'grp'), parts along dimension 1
- grad_down_cross: float32 [4, 5120, 2560], P(None, 'feat', 'grp'), parts along dimension 2
- grad_down_left: float32 [5120, 256], P('feat', 'grp'), parts along dimension 1
- grad_down_right: float32 [20480, 256], P('feat', 'grp'), parts along dimension 1
There are 2 independent parts, one for each index of `grp`. A program takes and returns all parts, laid end to end along the dimension named above; an argument that names none is the same for every part. Nothing has to cross between parts.
All inputs are finite; a program needn't handle non-finite values. No bound on the sum of `pattern` on one device may be relied on, other than what follows from the above.
Results may differ from a plain program's by a relative error of at most 0.0062.
Values may be sent and summed in bfloat16 or wider, within the bound.
A program may use at most 320 MiB of HBM per device.

v0:
```python
import jax
import jax.numpy as jnp
from jax import lax
from jax.sharding import PartitionSpec as P


def swapped(block, axis, apart):
    count = lax.axis_size(axis)
    route = []
    for low in range(count):
        high = low | 1 << apart
        if high != low and high < count:
            route += [(low, high), (high, low)]
    return lax.ppermute(block, axis, route)


def activate(values):
    return jax.nn.gelu(values, approximate=True)


def across(left, right):
    return lax.dot_general(
        left, right, (((0,), (0,)), ((), ())), preferred_element_type=jnp.float32
    )


def against(left, right):
    return lax.dot_general(
        left, right, (((1,), (1,)), ((), ())), preferred_element_type=jnp.float32
    )


def on_device(
    inputs,
    pattern,
    rank_mask,
    up_diag,
    up_cross,
    up_left,
    up_right,
    down_diag,
    down_cross,
    down_left,
    down_right,
    cotangent,
):
    levels = up_cross.shape[0]
    highest = lax.axis_size("feat").bit_length() - 1
    level_bits = [highest - levels + level for level in range(levels)]
    gate_values = pattern.astype(jnp.float32)
    gate_blocks = pattern.astype(jnp.bfloat16)[:, :, None]
    up_gated = up_cross * gate_blocks
    down_gated = down_cross * gate_blocks
    keep = rank_mask.astype(jnp.float32)[:, None]
    inputs_far = []
    up_far = []
    down_far = []
    for level in range(levels):
        received = swapped((inputs, up_gated[level], down_gated[level]), "feat", level_bits[level])
        inputs_far.append(received[0])
        up_far.append(received[1])
        down_far.append(received[2])
    pre_act = jnp.dot(up_diag, inputs, preferred_element_type=jnp.float32)
    for level in range(levels):
        pre_act = pre_act + jnp.dot(
            up_gated[level], inputs_far[level], preferred_element_type=jnp.float32
        )
    up_code = (lax.psum(across(up_right, inputs), "feat") * keep).astype(jnp.bfloat16)
    pre_act = pre_act + jnp.dot(up_left, up_code, preferred_element_type=jnp.float32)
    hidden = activate(pre_act).astype(jnp.bfloat16)
    result = jnp.dot(down_diag, hidden, preferred_element_type=jnp.float32)
    hidden_far = []
    for level in range(levels):
        neighbour = swapped(hidden, "feat", level_bits[level])
        hidden_far.append(neighbour)
        result = result + jnp.dot(down_gated[level], neighbour, preferred_element_type=jnp.float32)
    down_code = (lax.psum(across(down_right, hidden), "feat") * keep).astype(jnp.bfloat16)
    result = result + jnp.dot(down_left, down_code, preferred_element_type=jnp.float32)
    output = result.astype(jnp.bfloat16)
    down_back = (lax.psum(across(down_left, cotangent), "feat") * keep).astype(jnp.bfloat16)
    hidden_grad = across(down_diag, cotangent) + jnp.dot(
        down_right, down_back, preferred_element_type=jnp.float32
    )
    down_cross_grads = []
    for level in range(levels):
        far_cot = swapped(cotangent, "feat", level_bits[level])
        hidden_grad = hidden_grad + across(down_far[level], far_cot)
        down_cross_grads.append(gate_values[level, 0] * against(cotangent, hidden_far[level]))
    pre_grad = jax.vjp(activate, pre_act)[1](hidden_grad)[0].astype(jnp.bfloat16)
    up_back = (lax.psum(across(up_left, pre_grad), "feat") * keep).astype(jnp.bfloat16)
    in_grad = across(up_diag, pre_grad) + jnp.dot(
        up_right, up_back, preferred_element_type=jnp.float32
    )
    for level in range(levels):
        far_grad = swapped(pre_grad, "feat", level_bits[level])
        in_grad = in_grad + across(up_far[level], far_grad)
    input_grad = in_grad.astype(jnp.bfloat16)
    grad_up_diag = against(pre_grad, inputs)
    grad_up_cross = jnp.stack(
        [gate_values[level, 0] * against(pre_grad, inputs_far[level]) for level in range(levels)]
    )
    grad_up_left = against(pre_grad, up_code)
    grad_up_right = against(inputs, up_back)
    grad_down_diag = against(cotangent, hidden)
    grad_down_cross = jnp.stack(down_cross_grads)
    grad_down_left = against(cotangent, down_code)
    grad_down_right = against(hidden, down_back)
    return (
        output,
        input_grad,
        grad_up_diag,
        grad_up_cross,
        grad_up_left,
        grad_up_right,
        grad_down_diag,
        grad_down_cross,
        grad_down_left,
        grad_down_right,
    )


def solution(mesh):
    in_specs = (
        P("feat", "grp"),
        P(None, "feat"),
        P(),
        P("feat", None),
        P(None, "feat", None),
        P("feat", None),
        P("feat", None),
        P("feat", None),
        P(None, "feat", None),
        P("feat", None),
        P("feat", None),
        P("feat", "grp"),
    )
    out_specs = (
        P("feat", "grp"),
        P("feat", "grp"),
        P("feat", "grp"),
        P(None, "feat", "grp"),
        P("feat", "grp"),
        P("feat", "grp"),
        P("feat", "grp"),
        P(None, "feat", "grp"),
        P("feat", "grp"),
        P("feat", "grp"),
    )
    return jax.shard_map(
        on_device, mesh=mesh, in_specs=in_specs, out_specs=out_specs, check_vma=False
    )
```

profile of v0, /device:TPU:0, one launch (start us, length us, event | category | flops | bytes accessed | tf_op | source)
XLA Modules:
  0.0 959.8 jit_solution(9010921354594521081)
XLA Ops:
  7.8 2.6 collective-permute-start.11
  12.6 2.8 fusion.43
  28.0 5.5 fusion.42
  33.5 5.7 fusion.44
  39.9 84.3 %all-reduce.7.cloned.1.call-done = (f32[128,2048]{1,0:T(8,128)}, f32[128,2048]{1,0:T(8,128)}) async-done(((f32[128,2048]{1,0:T(8,128)}, f32[128,2048]{1,0:T(8,128)}), (f32[128,2048]{1,0:T(8,128)}, f32[128,2048]{1,0:T(8,128)})) %all-reduce.7.cloned.1.call-update) | async-done | bytes 2097168 | tf_op jit(solution)/shard_map/psum | solution.py:68
  124.2 6.9 fusion.30
  131.1 5.5 fusion.32
  138.2 6.8 fusion.33
  145.1 6.9 fusion.34
  153.0 6.8 fusion.35
  162.5 6.8 fusion.46
  169.3 3.4 collective-permute-done.10
  175.6 7.2 fusion.47
  182.8 30.3 %collective-permute-done.12 = bf16[320,1280]{1,0:T(8,128)(2,1)S(1)} collective-permute-done((bf16[320,1280]{1,0:T(8,128)(2,1)S(1)}, bf16[320,1280]{1,0:T(8,128)(2,1)S(1)}, u32[]{:S(2)}, u32[]{:S(2)}) %collective-permute-start.12) | collective-permute-done | bytes 819232 | tf_op jit(solution)/shard_map/ppermute | solution.py:14
  213.1 5.5 fusion.48
  218.6 92.4 %collective-permute-done.14 = bf16[320,1280]{1,0:T(8,128)(2,1)S(1)} collective-permute-done((bf16[320,1280]{1,0:T(8,128)(2,1)S(1)}, bf16[320,1280]{1,0:T(8,128)(2,1)S(1)}, u32[]{:S(2)}, u32[]{:S(2)}) %collective-permute-start.14) | collective-permute-done | bytes 819232 | tf_op jit(solution)/shard_map/ppermute | solution.py:14
  311.0 5.7 fusion.49
  316.7 41.7 %fusion.6 = (bf16[1280,2048]{1,0:T(8,128)(2,1)}, bf16[1280,2048]{1,0:T(8,128)(2,1)}) fusion(f32[1280,2048]{1,0:T(8,128)} %fusion.49, f32[1280,2048]{1,0:T(8,128)} %fusion.48, f32[1280,2048]{1,0:T(8,128)} %fusion.47, f32[1280,2048]{1,0:T(8,128)} %fusion.46, f32[1280,2048]{1,0:T(8,128)} %fusion.44, f32[2048,1280]{0,1:T(8,128)} %fusion.32, ...), kind=kOutput, calls=%fused_computation.8 | convolution fusion | flops 1761607680 | bytes 127959040 | tf_op jit(solution)/shard_map/dot_general | solution.py:65
  359.7 2.5 collective-permute-start.7
  362.1 4.4 convolution_bitcast_fusion.4
  366.5 4.4 convolution_bitcast_fusion.3
  370.9 5.9 fusion.54
  377.8 5.7 fusion.12
  383.6 5.5 fusion.11
  389.1 3.4 convolution_bitcast_fusion
  392.5 5.5 fusion.13
  398.0 5.3 fusion.14
  403.3 3.2 pad_maximum_fusion
  406.6 5.6 fusion.53
  412.2 4.9 fusion.29
  417.1 3.1 convolution_bitcast_fusion.1
  422.7 245.8 %all-reduce.5.cloned.1.call-done = (f32[128,2048]{1,0:T(8,128)}, f32[128,2048]{1,0:T(8,128)}) async-done(((f32[128,2048]{1,0:T(8,128)}, f32[128,2048]{1,0:T(8,128)}), (f32[128,2048]{1,0:T(8,128)}, f32[128,2048]{1,0:T(8,128)})) %all-reduce.5.cloned.1.call-update) | async-done | bytes 2097168 | tf_op jit(solution)/shard_map/psum | solution.py:77
  668.5 2.6 convolution_bitcast_fusion.5
  677.8 4.4 fusion.37
  682.3 5.0 fusion.16
  687.3 5.3 fusion.17
  692.7 4.4 fusion.38
  697.1 5.0 fusion.18
  703.1 5.9 fusion.39
  709.0 5.1 fusion.15
  714.1 8.7 collective-permute-done.18
  724.8 4.4 fusion.50
  729.2 3.3 pad_maximum_fusion.1
  732.5 201.0 %collective-permute-done.20 = bf16[1280,320]{0,1:T(8,128)(2,1)S(1)} collective-permute-done((bf16[1280,320]{0,1:T(8,128)(2,1)S(1)}, bf16[1280,320]{0,1:T(8,128)(2,1)S(1)}, u32[]{:S(2)}, u32[]{:S(2)}) %collective-permute-start.20) | collective-permute-done | bytes 819232 | tf_op jit(solution)/shard_map/ppermute | solution.py:14
  935.4 2.8 collective-permute-done.22
  938.1 4.4 fusion.52
  942.5 6.8 fusion.27
  949.4 3.1 fusion.28
  (124 shorter events, 40.5 us)
Async XLA Ops:
  7.2 20.8 %copy-start = (bf16[1280,320]{0,1:T(8,128)(2,1)S(1)}, bf16[1280,320]{0,1:T(8,128)(2,1)}, u32[]{:S(2)}) copy-start(bf16[1280,320]{0,1:T(8,128)(2,1)} %param.15) | copy-start | bytes 2457604
  7.2 8.3 copy-start.7
  7.2 10.7 %copy-start.29 = (s32[4,1]{0,1:T(1,128)S(1)}, s32[4,1]{0,1:T(1,128)}, u32[]{:S(2)}) copy-start(s32[4,1]{0,1:T(1,128)} %param.13) | copy-start | bytes 52
  7.2 116.9 %all-reduce.7.cloned.1.call-start = ((), (), s32[]{:S(2)}) async-start(), calls=%async_computation.1 | async-start | bytes 4194304 | tf_op jit(solution)/shard_map/psum | solution.py:68
  7.3 154.0 %collective-permute-start.9 = (bf16[320,2048]{1,0:T(8,128)(2,1)}, bf16[320,2048]{1,0:T(8,128)(2,1)}, u32[]{:S(2)}, u32[]{:S(2)}) collective-permute-start(bf16[320,2048]{1,0:T(8,128)(2,1)} %param.23), channel_id=1, source_target_pairs={{0,1},{1,0},{2,3},{3,2},{4,5},{5,4},{6,7},{7,6},{8,9},{9,8},{10,11... | collective-permute-start | bytes 3932168 | tf_op jit(solution)/shard_map/ppermute | solution.py:14
  7.8 166.4 %collective-permute-start.11 = (bf16[320,2048]{1,0:T(8,128)(2,1)}, bf16[320,2048]{1,0:T(8,128)(2,1)}, u32[]{:S(2)}, u32[]{:S(2)}) collective-permute-start(bf16[320,2048]{1,0:T(8,128)(2,1)} %param.23), channel_id=1, source_target_pairs={{0,2},{2,0},{1,3},{3,1},{4,6},{6,4},{5,7},{7,5},{8,10},{10,8},{9,1... | collective-permute-start | bytes 3932168 | tf_op jit(solution)/shard_map/ppermute | solution.py:14
  10.4 126.2 %collective-permute-start = (bf16[320,2048]{1,0:T(8,128)(2,1)}, bf16[320,2048]{1,0:T(8,128)(2,1)}, u32[]{:S(2)}, u32[]{:S(2)}) collective-permute-start(bf16[320,2048]{1,0:T(8,128)(2,1)} %param.12), channel_id=1, source_target_pairs={{0,1},{1,0},{2,3},{3,2},{4,5},{5,4},{6,7},{7,6},{8,9},{9,8},{10,11... | collective-permute-start | bytes 3932168 | tf_op jit(solution)/shard_map/ppermute | solution.py:14
  10.5 134.5 %collective-permute-start.1 = (bf16[320,2048]{1,0:T(8,128)(2,1)}, bf16[320,2048]{1,0:T(8,128)(2,1)}, u32[]{:S(2)}, u32[]{:S(2)}) collective-permute-start(bf16[320,2048]{1,0:T(8,128)(2,1)} %param.12), channel_id=1, source_target_pairs={{0,2},{2,0},{1,3},{3,1},{4,6},{6,4},{5,7},{7,5},{8,10},{10,8},{9,1... | collective-permute-start | bytes 3932168 | tf_op jit(solution)/shard_map/ppermute | solution.py:14
  10.8 141.2 %collective-permute-start.2 = (bf16[320,2048]{1,0:T(8,128)(2,1)}, bf16[320,2048]{1,0:T(8,128)(2,1)}, u32[]{:S(2)}, u32[]{:S(2)}) collective-permute-start(bf16[320,2048]{1,0:T(8,128)(2,1)} %param.12), channel_id=1, source_target_pairs={{0,4},{4,0},{1,5},{5,1},{2,6},{6,2},{3,7},{7,3},{8,12},{12,8},{9,1... | collective-permute-start | bytes 3932168 | tf_op jit(solution)/shard_map/ppermute | solution.py:14
  17.8 650.6 %all-reduce.5.cloned.1.call-start = ((), (), s32[]{:S(2)}) async-start(), calls=%async_computation | async-start | bytes 4194304 | tf_op jit(solution)/shard_map/psum | solution.py:77
  33.5 5.7 copy-start.30
  124.2 6.9 copy-start.9
  124.2 6.9 copy-start.15
  131.1 7.1 copy-start.3
  136.6 8.4 copy-start.26
  136.6 76.5 %collective-permute-start.13 = (bf16[320,2048]{1,0:T(8,128)(2,1)S(1)}, bf16[320,2048]{1,0:T(8,128)(2,1)S(1)}, u32[]{:S(2)}, u32[]{:S(2)}) collective-permute-start(bf16[320,2048]{1,0:T(8,128)(2,1)S(1)} %copy-done.7), channel_id=1, source_target_pairs={{0,4},{4,0},{1,5},{5,1},{2,6},{6,2},{3,7},{7,3},{8,12},{12,8},{9,1... | collective-permute-start | bytes 3932168 | tf_op jit(solution)/shard_map/ppermute | solution.py:14
  145.0 7.0 copy-start.25
  145.0 14.8 %collective-permute-start.8 = (bf16[320,1280]{1,0:T(8,128)(2,1)S(1)}, bf16[320,1280]{1,0:T(8,128)(2,1)S(1)}, u32[]{:S(2)}, u32[]{:S(2)}) collective-permute-start(bf16[320,1280]{1,0:T(8,128)(2,1)S(1)} %copy-done.26), channel_id=1, source_target_pairs={{0,1},{1,0},{2,3},{3,2},{4,5},{5,4},{6,7},{7,6},{8,9},{9,8},{10,11... | collective-permute-start | bytes 2457608 | tf_op jit(solution)/shard_map/ppermute | solution.py:14
  152.0 9.3 copy-start.24
  152.0 20.7 %collective-permute-start.10 = (bf16[320,1280]{1,0:T(8,128)(2,1)S(1)}, bf16[320,1280]{1,0:T(8,128)(2,1)S(1)}, u32[]{:S(2)}, u32[]{:S(2)}) collective-permute-start(bf16[320,1280]{1,0:T(8,128)(2,1)S(1)} %copy-done.25), channel_id=1, source_target_pairs={{0,2},{2,0},{1,3},{3,1},{4,6},{6,4},{5,7},{7,5},{8,10},{10,8},{9,1... | collective-permute-start | bytes 2457608 | tf_op jit(solution)/shard_map/ppermute | solution.py:14
  159.8 151.2 %collective-permute-start.15 = (bf16[320,2048]{1,0:T(8,128)(2,1)S(1)}, bf16[320,2048]{1,0:T(8,128)(2,1)S(1)}, u32[]{:S(2)}, u32[]{:S(2)}) collective-permute-start(bf16[320,2048]{1,0:T(8,128)(2,1)S(1)} %copy-done.7), channel_id=1, source_target_pairs={{0,8},{8,0},{1,9},{9,1},{2,10},{10,2},{3,11},{11,3},{4,12},{12,4},... | collective-permute-start | bytes 3932168 | tf_op jit(solution)/shard_map/ppermute | solution.py:14
  161.3 12.9 %copy-start.23 = (bf16[320,1280]{1,0:T(8,128)(2,1)S(1)}, bf16[320,1280]{1,0:T(8,128)(2,1)}, u32[]{:S(2)}) copy-start(bf16[320,1280]{1,0:T(8,128)(2,1)} %get-tuple-element.21) | copy-start | bytes 2457604
  161.3 51.8 %collective-permute-start.12 = (bf16[320,1280]{1,0:T(8,128)(2,1)S(1)}, bf16[320,1280]{1,0:T(8,128)(2,1)S(1)}, u32[]{:S(2)}, u32[]{:S(2)}) collective-permute-start(bf16[320,1280]{1,0:T(8,128)(2,1)S(1)} %copy-done.24), channel_id=1, source_target_pairs={{0,4},{4,0},{1,5},{5,1},{2,6},{6,2},{3,7},{7,3},{8,12},{12,8},{9,1... | collective-permute-start | bytes 2457608 | tf_op jit(solution)/shard_map/ppermute | solution.py:14
  172.7 144.0 %collective-permute-start.3 = (bf16[320,2048]{1,0:T(8,128)(2,1)S(1)}, bf16[320,2048]{1,0:T(8,128)(2,1)}, u32[]{:S(2)}, u32[]{:S(2)}) collective-permute-start(bf16[320,2048]{1,0:T(8,128)(2,1)S(1)} %copy-done.6), channel_id=1, source_target_pairs={{0,8},{8,0},{1,9},{9,1},{2,10},{10,2},{3,11},{11,3},{4,12},{12,4},... | collective-permute-start | bytes 3932168 | tf_op jit(solution)/shard_map/ppermute | solution.py:14
  174.1 136.9 %collective-permute-start.14 = (bf16[320,1280]{1,0:T(8,128)(2,1)S(1)}, bf16[320,1280]{1,0:T(8,128)(2,1)S(1)}, u32[]{:S(2)}, u32[]{:S(2)}) collective-permute-start(bf16[320,1280]{1,0:T(8,128)(2,1)S(1)} %copy-done.23), channel_id=1, source_target_pairs={{0,8},{8,0},{1,9},{9,1},{2,10},{10,2},{3,11},{11,3},{4,12},{12,4},... | collective-permute-start | bytes 2457608 | tf_op jit(solution)/shard_map/ppermute | solution.py:14
  358.4 8.1 copy-start.16
  358.4 343.7 %collective-permute-start.4 = (bf16[1280,2048]{1,0:T(8,128)(2,1)}, bf16[1280,2048]{1,0:T(8,128)(2,1)}, u32[]{:S(2)}, u32[]{:S(2)}) collective-permute-start(bf16[1280,2048]{1,0:T(8,128)(2,1)} %get-tuple-element.15), channel_id=1, source_target_pairs={{0,1},{1,0},{2,3},{3,2},{4,5},{5,4},{6,7},{7,6},{8,9},{9,8},{10,11... | collective-permute-start | bytes 15728648 | tf_op jit(solution)/shard_map/ppermute | solution.py:14
  358.5 315.0 %collective-permute-start.5 = (bf16[1280,2048]{1,0:T(8,128)(2,1)}, bf16[1280,2048]{1,0:T(8,128)(2,1)}, u32[]{:S(2)}, u32[]{:S(2)}) collective-permute-start(bf16[1280,2048]{1,0:T(8,128)(2,1)} %get-tuple-element.15), channel_id=1, source_target_pairs={{0,2},{2,0},{1,3},{3,1},{4,6},{6,4},{5,7},{7,5},{8,10},{10,8},{9,1... | collective-permute-start | bytes 15728648 | tf_op jit(solution)/shard_map/ppermute | solution.py:14
  359.7 316.8 %collective-permute-start.6 = (bf16[1280,2048]{1,0:T(8,128)(2,1)}, bf16[1280,2048]{1,0:T(8,128)(2,1)}, u32[]{:S(2)}, u32[]{:S(2)}) collective-permute-start(bf16[1280,2048]{1,0:T(8,128)(2,1)} %get-tuple-element.15), channel_id=1, source_target_pairs={{0,4},{4,0},{1,5},{5,1},{2,6},{6,2},{3,7},{7,3},{8,12},{12,8},{9,1... | collective-permute-start | bytes 15728648 | tf_op jit(solution)/shard_map/ppermute | solution.py:14
  359.7 332.9 %collective-permute-start.7 = (bf16[1280,2048]{1,0:T(8,128)(2,1)}, bf16[1280,2048]{1,0:T(8,128)(2,1)}, u32[]{:S(2)}, u32[]{:S(2)}) collective-permute-start(bf16[1280,2048]{1,0:T(8,128)(2,1)} %get-tuple-element.15), channel_id=1, source_target_pairs={{0,8},{8,0},{1,9},{9,1},{2,10},{10,2},{3,11},{11,3},{4,12},{12,4},... | collective-permute-start | bytes 15728648 | tf_op jit(solution)/shard_map/ppermute | solution.py:14
  376.8 347.1 %collective-permute-start.19 = (bf16[1280,2048]{1,0:T(8,128)(2,1)}, bf16[1280,2048]{1,0:T(8,128)(2,1)}, u32[]{:S(2)}, u32[]{:S(2)}) collective-permute-start(bf16[1280,2048]{1,0:T(8,128)(2,1)} %get-tuple-element.14), channel_id=1, source_target_pairs={{0,2},{2,0},{1,3},{3,1},{4,6},{6,4},{5,7},{7,5},{8,10},{10,8},{9,1... | collective-permute-start | bytes 15728648 | tf_op jit(solution)/shard_map/ppermute | solution.py:14
  377.8 11.3 %slice-start = ((s8[5242880]{0:T(1024)(128)(4,1)}), s8[4194304]{0:T(1024)(128)(4,1)S(1)}, s32[]{:S(2)}) async-start(s8[5242880]{0:T(1024)(128)(4,1)} %bitcast.160), calls=%async_computation.2 | async-start | bytes 8388608
  383.5 5.6 slice-start.1
  383.6 5.6 copy-start.18
  406.5 5.6 copy-start.11
  420.2 250.9 %copy-start.27 = (bf16[320,128]{1,0:T(8,128)(2,1)S(1)}, bf16[320,128]{1,0:T(8,128)(2,1)}, u32[]{:S(2)}) copy-start(bf16[320,128]{1,0:T(8,128)(2,1)} %param.21) | copy-start | bytes 245764
  422.7 250.2 %copy-start.28 = (bf16[320,128]{1,0:T(8,128)(2,1)S(1)}, bf16[320,128]{1,0:T(8,128)(2,1)}, u32[]{:S(2)}) copy-start(bf16[320,128]{1,0:T(8,128)(2,1)} %param.18) | copy-start | bytes 245764
  673.5 260.0 %collective-permute-start.21 = (bf16[1280,2048]{1,0:T(8,128)(2,1)}, bf16[1280,2048]{1,0:T(8,128)(2,1)S(1)}, u32[]{:S(2)}, u32[]{:S(2)}) collective-permute-start(bf16[1280,2048]{1,0:T(8,128)(2,1)} %get-tuple-element.14), channel_id=1, source_target_pairs={{0,4},{4,0},{1,5},{5,1},{2,6},{6,2},{3,7},{7,3},{8,12},{12,8},{9,1... | collective-permute-start | bytes 15728648 | tf_op jit(solution)/shard_map/ppermute | solution.py:14
  676.4 261.7 %collective-permute-start.23 = (bf16[1280,2048]{1,0:T(8,128)(2,1)}, bf16[1280,2048]{1,0:T(8,128)(2,1)}, u32[]{:S(2)}, u32[]{:S(2)}) collective-permute-start(bf16[1280,2048]{1,0:T(8,128)(2,1)} %get-tuple-element.14), channel_id=1, source_target_pairs={{0,8},{8,0},{1,9},{9,1},{2,10},{10,2},{3,11},{11,3},{4,12},{12,4},... | collective-permute-start | bytes 15728648 | tf_op jit(solution)/shard_map/ppermute | solution.py:14
  692.6 256.8 %collective-permute-start.17 = (bf16[1280,2048]{1,0:T(8,128)(2,1)}, bf16[1280,2048]{1,0:T(8,128)(2,1)S(1)}, u32[]{:S(2)}, u32[]{:S(2)}) collective-permute-start(bf16[1280,2048]{1,0:T(8,128)(2,1)} %get-tuple-element.14), channel_id=1, source_target_pairs={{0,1},{1,0},{2,3},{3,2},{4,5},{5,4},{6,7},{7,6},{8,9},{9,8},{10,11... | collective-permute-start | bytes 15728648 | tf_op jit(solution)/shard_map/ppermute | solution.py:14
  702.1 20.7 %collective-permute-start.18 = (bf16[1280,320]{0,1:T(8,128)(2,1)S(1)}, bf16[1280,320]{0,1:T(8,128)(2,1)S(1)}, u32[]{:S(2)}, u32[]{:S(2)}) collective-permute-start(bf16[1280,320]{0,1:T(8,128)(2,1)S(1)} %copy-done.22), channel_id=1, source_target_pairs={{0,2},{2,0},{1,3},{3,1},{4,6},{6,4},{5,7},{7,5},{8,10},{10,8},{9,1... | collective-permute-start | bytes 2457608 | tf_op jit(solution)/shard_map/ppermute | solution.py:14
  709.0 13.8 %copy-start.21 = (bf16[1280,320]{0,1:T(8,128)(2,1)S(1)}, bf16[1280,320]{0,1:T(8,128)(2,1)}, u32[]{:S(2)}) copy-start(bf16[1280,320]{0,1:T(8,128)(2,1)} %get-tuple-element.18) | copy-start | bytes 2457604
  709.0 14.9 %copy-start.20 = (bf16[1280,320]{0,1:T(8,128)(2,1)S(1)}, bf16[1280,320]{0,1:T(8,128)(2,1)}, u32[]{:S(2)}) copy-start(bf16[1280,320]{0,1:T(8,128)(2,1)} %get-tuple-element.17) | copy-start | bytes 2457604
  722.8 210.7 %collective-permute-start.20 = (bf16[1280,320]{0,1:T(8,128)(2,1)S(1)}, bf16[1280,320]{0,1:T(8,128)(2,1)S(1)}, u32[]{:S(2)}, u32[]{:S(2)}) collective-permute-start(bf16[1280,320]{0,1:T(8,128)(2,1)S(1)} %copy-done.21), channel_id=1, source_target_pairs={{0,4},{4,0},{1,5},{5,1},{2,6},{6,2},{3,7},{7,3},{8,12},{12,8},{9,1... | collective-permute-start | bytes 2457608 | tf_op jit(solution)/shard_map/ppermute | solution.py:14
  723.9 214.3 %collective-permute-start.22 = (bf16[1280,320]{0,1:T(8,128)(2,1)S(1)}, bf16[1280,320]{0,1:T(8,128)(2,1)S(1)}, u32[]{:S(2)}, u32[]{:S(2)}) collective-permute-start(bf16[1280,320]{0,1:T(8,128)(2,1)S(1)} %copy-done.20), channel_id=1, source_target_pairs={{0,8},{8,0},{1,9},{9,1},{2,10},{10,2},{3,11},{11,3},{4,12},{12,4},... | collective-permute-start | bytes 2457608 | tf_op jit(solution)/shard_map/ppermute | solution.py:14
  729.2 204.3 %copy-start.19 = (bf16[1280,320]{0,1:T(8,128)(2,1)S(1)}, bf16[1280,320]{0,1:T(8,128)(2,1)}, u32[]{:S(2)}) copy-start(bf16[1280,320]{0,1:T(8,128)(2,1)} %get-tuple-element.16) | copy-start | bytes 2457604
  933.5 15.9 %collective-permute-start.16 = (bf16[1280,320]{0,1:T(8,128)(2,1)S(1)}, bf16[1280,320]{0,1:T(8,128)(2,1)S(1)}, u32[]{:S(2)}, u32[]{:S(2)}) collective-permute-start(bf16[1280,320]{0,1:T(8,128)(2,1)S(1)} %copy-done.19), channel_id=1, source_target_pairs={{0,1},{1,0},{2,3},{3,2},{4,5},{5,4},{6,7},{7,6},{8,9},{9,8},{10,11... | collective-permute-start | bytes 2457608 | tf_op jit(solution)/shard_map/ppermute | solution.py:14
  935.4 7.1 copy-start.12
  (11 other events, 41.0 us)
Sparse Core Ops, SparseCore 0:
  17.9 106.1 all-reduce.6
  377.9 290.4 all-reduce.4
where the time goes:
time: 970 us; the launch traced here: 960 us
  waiting for transfers between devices  669 us (69%)
  matrix products  234 us (24%)
  starting transfers between devices  24.4 us (3%)
  between operations  15 us (2%)
    ppermute x24, waiting for transfers between devices, swapped(): return lax.ppermute(block, axis, route)  339 us
    psum x1, waiting for transfers between devices, on_device(): lax.psum(across(down_right, hidden), 'feat') * keep  246 us
    psum x1, waiting for transfers between devices, on_device(): lax.psum(across(up_right, inputs), 'feat') * keep  84.3 us
    dot_general x14, matrix products, across(): lax.dot_general(left, right, (((0,), (0,)), ((), ())), preferred_element_...  64.4 us
    dot_general x14, matrix products, against(): lax.dot_general(left, right, (((1,), (1,)), ((), ())), preferred_element_...  62.4 us
    dot_general x4, matrix products, on_device(): jnp.dot(up_gated[level], inputs_far[level], preferred_element_type=jnp.fl...  62.3 us
    ppermute x24, starting transfers between devices, swapped(): return lax.ppermute(block, axis, route)  24.3 us
    dot_general x4, matrix products, on_device(): jnp.dot(down_gated[level], neighbour, preferred_element_type=jnp.float32)  21.6 us
  transfers between devices with their start and end apart: 26, of which 8 were waited for; matrix products, arithmetic and copies ran while one was open for 21% of the time, Pallas kernels for 0%

commit v1 on v0

v1 whole, which is shorter than its diff:
```python
import functools

import jax
import jax.numpy as jnp
from jax import lax
from jax.experimental import pallas as pl
from jax.experimental.pallas import tpu as pltpu
from jax.sharding import PartitionSpec as P


def swapped(block, axis, apart):
    count = lax.axis_size(axis)
    route = []
    for low in range(count):
        high = low | 1 << apart
        if high != low and high < count:
            route += [(low, high), (high, low)]
    return lax.ppermute(block, axis, route)


def after(block, *earlier):
    return lax.optimization_barrier((block,) + earlier)[0]


def outer(total, left, right, by_column):
    extent = (right if by_column else left)[0].shape[0]
    tile = 256 if extent % 256 == 0 else extent

    def step(index, carry):
        span = pl.ds(pl.multiple_of(index * tile, tile), tile)
        value = None
        for one, two in zip(left, right):
            term = against(one[...], two[span]) if by_column else against(one[span], two[...])
            value = term if value is None else value + term
        if by_column:
            total[:, span] = value
        else:
            total[span] = value
        return carry

    lax.fori_loop(0, extent // tile, step, 0)


def chunk_kernel(level_bits, columns, feats, earlier, *refs):
    blocks = len(columns)
    levels = len(level_bits)
    sources, refs = refs[:blocks], refs[blocks:]
    stored, refs = refs[: 6 + earlier], refs[6 + earlier :]
    landing, refs = refs[:blocks], refs[blocks:]
    hidden, pre_grad, out_near, in_near, payload, code = refs[:6]
    refs = refs[6:]
    if earlier:
        grads, refs = refs[0], refs[1:]
    loaded = refs[: 6 + earlier]
    far_send, far_recv, local = refs[6 + earlier :]
    up, up_turned, down, down_turned, ins, cots = loaded[:6]
    place = lax.axis_index("feat")
    width = ins.shape[1]
    code_rows = feats * (levels + 1)
    rank = ins.shape[0] - code_rows
    partners = []
    for bit in level_bits:
        mine = lax.rem(place // (1 << bit), 2)
        partners.append(place + (1 - 2 * mine) * (1 << bit))
    loads = []
    for index, (source, target) in enumerate(zip(stored, loaded)):
        copy = pltpu.make_async_copy(source, target, local.at[index])
        copy.start()
        loads.append(copy)
    barrier = pltpu.get_barrier_semaphore()
    for partner in partners:
        pl.semaphore_signal(
            barrier, inc=1, device_id={"feat": partner}, device_id_type=pl.DeviceIdType.MESH
        )
    pl.semaphore_wait(barrier, levels)
    started = []
    for index, (start, size) in enumerate(columns):
        for level in reversed(range(levels)):
            source = sources[index]
            if len(source.shape) == 3:
                source = source.at[level]
            spot = index * levels + level
            copy = pltpu.make_async_remote_copy(
                src_ref=source.at[:, start : start + size],
                dst_ref=landing[index].at[level],
                send_sem=far_send.at[spot],
                recv_sem=far_recv.at[spot],
                device_id={"feat": partners[level]},
                device_id_type=pl.DeviceIdType.MESH,
            )
            copy.start()
            started.append(copy)
    for copy in loads:
        copy.wait()
    tile = 256 if width % 256 == 0 else width

    def step(index, carry):
        span = pl.ds(pl.multiple_of(index * tile, tile), tile)
        later = pl.ds(pl.multiple_of(width + index * tile, tile), tile)
        active, slope = activate(dot(up[...], ins[:, span]))
        active = active.astype(jnp.bfloat16)
        hidden[:, span] = active
        outs = dot(down[...], active)
        grad = (dot(down_turned[...], cots[:, span]) * slope).astype(jnp.bfloat16)
        pre_grad[:, span] = grad
        in_grads = dot(up_turned[...], grad)
        out_near[:, span] = outs[:feats]
        in_near[:, span] = in_grads[:feats]
        for level in range(levels):
            rows = slice(feats * (level + 1), feats * (level + 2))
            payload[level, :, span] = outs[rows].astype(jnp.bfloat16)
            payload[level, :, later] = in_grads[rows].astype(jnp.bfloat16)
        code[:rank, span] = outs[code_rows:]
        code[rank:, span] = in_grads[code_rows:]
        return carry

    lax.fori_loop(0, width // tile, step, 0)
    if earlier:
        outer(grads, (loaded[6], cots), (loaded[7], hidden), True)
    for copy in started:
        copy.wait()


def chunk_step(level_bits, blocks, stored, feats, number):
    levels = len(level_bits)
    hid = stored[0].shape[0]
    rows, width = stored[4].shape
    rank = rows - feats * (levels + 1)
    earlier = len(stored) - 6
    copies = len(blocks) * levels
    made = [
        ((hid, width), jnp.bfloat16),
        ((hid, width), jnp.bfloat16),
        ((feats, width), jnp.float32),
        ((feats, width), jnp.float32),
        ((levels, feats, 2 * width), jnp.bfloat16),
        ((2 * rank, width), jnp.float32),
    ]
    if earlier:
        made.append(((rows, hid), jnp.float32))
    found = pl.pallas_call(
        functools.partial(
            chunk_kernel, tuple(level_bits), tuple(block[1:] for block in blocks), feats, earlier
        ),
        out_shape=[
            jax.ShapeDtypeStruct((levels, block.shape[-2], size), block.dtype)
            for block, _, size in blocks
        ]
        + [jax.ShapeDtypeStruct(*one) for one in made],
        in_specs=[pl.BlockSpec(memory_space=pl.ANY)] * (len(blocks) + len(stored)),
        out_specs=[pl.BlockSpec(memory_space=pl.ANY)] * len(blocks)
        + [pl.BlockSpec(memory_space=pltpu.VMEM)] * len(made),
        scratch_shapes=[pltpu.VMEM(block.shape, block.dtype) for block in stored]
        + [
            pltpu.SemaphoreType.DMA((copies,)),
            pltpu.SemaphoreType.DMA((copies,)),
            pltpu.SemaphoreType.DMA((len(stored),)),
        ],
        compiler_params=pltpu.CompilerParams(
            collective_id=number, has_side_effects=True, vmem_limit_bytes=60 * 2**20
        ),
    )(*[block[0] for block in blocks], *stored)
    return found[: len(blocks)], found[len(blocks) :]


def exchange_kernel(level_bits, sizes, early, pairs, part, *refs):
    blocks = len(sizes)
    levels = len(level_bits)
    sources, refs = refs[:blocks], refs[blocks:]
    stored, refs = refs[:pairs], refs[pairs:]
    code, landing, refs = refs[0], refs[1 : blocks + 1], refs[blocks + 1 :]
    if pairs:
        grads, refs = refs[0], refs[1:]
    work, received, gathered, send, recv, far_send, far_recv = refs[:7]
    loaded = refs[7 : 7 + pairs]
    count = part.shape[0]
    bits = count.bit_length() - 1
    place = lax.axis_index("feat")

    def partner(bit):
        mine = lax.rem(place // (1 << bit), 2)
        return mine, place + (1 - 2 * mine) * (1 << bit)

    def far(index, level):
        source = sources[index]
        if len(source.shape) == 3:
            source = source.at[level]
        spot = index * levels + level
        return pltpu.make_async_remote_copy(
            src_ref=source.at[:, : sizes[index]],
            dst_ref=landing[index].at[level],
            send_sem=far_send.at[spot],
            recv_sem=far_recv.at[spot],
            device_id={"feat": partner(level_bits[level])[1]},
            device_id_type=pl.DeviceIdType.MESH,
        )

    def near(source, target, step, bit):
        return pltpu.make_async_remote_copy(
            src_ref=source,
            dst_ref=target,
            send_sem=send.at[step],
            recv_sem=recv.at[step],
            device_id={"feat": partner(bit)[1]},
            device_id_type=pl.DeviceIdType.MESH,
        )

    barrier = pltpu.get_barrier_semaphore()
    for bit in range(bits):
        pl.semaphore_signal(
            barrier,
            inc=1,
            device_id={"feat": partner(bit)[1]},
            device_id_type=pl.DeviceIdType.MESH,
        )
    pl.semaphore_wait(barrier, bits)

    copies = []
    pending = [(index, level) for index in range(blocks) for level in reversed(range(levels))]
    started = []

    def launch(wanted):
        for item in list(pending):
            if wanted(*item):
                copy = far(*item)
                copy.start()
                started.append(copy)
                pending.remove(item)

    loads = [
        pltpu.make_async_copy(source, target, refs[-1].at[index])
        for index, (source, target) in enumerate(zip(stored, loaded))
    ]
    for copy in loads:
        copy.start()
    top = levels // 2
    launch(lambda index, level: index < early and level >= top)
    base = 0
    offset = 0
    length = count
    for bit in range(bits):
        mine = partner(bit)[0]
        half = length // 2
        keep = base + mine * half
        away = base + (1 - mine) * half
        held = part if bit == 0 else work
        copy = near(
            held.at[pl.ds(away, half)], received.at[pl.ds(offset, half)], bit, bit
        )
        copy.start()
        copies.append(copy)
        if bit == bits - levels + top:
            launch(lambda index, level: level < top)
        copy.wait_recv()
        work[pl.ds(keep, half)] = (
            held[pl.ds(keep, half)] + received[pl.ds(offset, half)]
        )
        base, offset, length = keep, offset + half, half
    launch(lambda index, level: index < early + 1)
    gathered[pl.ds(base, 1)] = work[pl.ds(base, 1)].astype(jnp.bfloat16)
    for bit in reversed(range(bits)):
        mine = partner(bit)[0]
        span = pl.ds(base, length)
        copy = near(gathered.at[span], gathered.at[span], 2 * bits - 1 - bit, bit)
        copy.start()
        copies.append(copy)
        copy.wait_recv()
        base, length = base - mine * length, 2 * length
        if bit == bits - levels + top:
            launch(lambda index, level: True)
    code[...] = gathered[...]
    for copy in loads:
        copy.wait()
    if pairs:
        outer(grads, loaded[: pairs // 2], loaded[pairs // 2 :], False)
    for copy in copies:
        copy.wait_send()
    for copy in started:
        copy.wait()


def exchange(part, level_bits, blocks, early, number, stored=()):
    count = lax.axis_size("feat")
    bits = count.bit_length() - 1
    levels = len(level_bits)
    flat = part.reshape(count, 16, -1)
    sizes = tuple(size for _, size in blocks)
    copies = max(1, len(blocks) * levels)
    found = pl.pallas_call(
        functools.partial(exchange_kernel, tuple(level_bits), sizes, early, len(stored)),
        out_shape=[jax.ShapeDtypeStruct(flat.shape, jnp.bfloat16)]
        + [
            jax.ShapeDtypeStruct((levels, block.shape[-2], size), block.dtype)
            for block, size in blocks
        ]
        + [
            jax.ShapeDtypeStruct((stored[0].shape[0], stored[-1].shape[0]), jnp.float32)
            for _ in stored[:1]
        ],
        in_specs=[pl.BlockSpec(memory_space=pltpu.VMEM)]
        + [pl.BlockSpec(memory_space=pl.ANY)] * (len(blocks) + len(stored)),
        out_specs=[pl.BlockSpec(memory_space=pltpu.VMEM)]
        + [pl.BlockSpec(memory_space=pl.ANY)] * len(blocks)
        + [pl.BlockSpec(memory_space=pltpu.VMEM) for _ in stored[:1]],
        scratch_shapes=[
            pltpu.VMEM(flat.shape, jnp.float32),
            pltpu.VMEM(flat.shape, jnp.float32),
            pltpu.VMEM(flat.shape, jnp.bfloat16),
            pltpu.SemaphoreType.DMA((2 * bits,)),
            pltpu.SemaphoreType.DMA((2 * bits,)),
            pltpu.SemaphoreType.DMA((copies,)),
            pltpu.SemaphoreType.DMA((copies,)),
        ]
        + [pltpu.VMEM(block.shape, block.dtype) for block in stored]
        + [pltpu.SemaphoreType.DMA((max(1, len(stored)),))],
        compiler_params=pltpu.CompilerParams(
            collective_id=number, has_side_effects=True, vmem_limit_bytes=56 * 2**20
        ),
    )(flat, *[block for block, _ in blocks], *stored)
    return found[0].reshape(part.shape), found[1:]


def activate(values):
    scale = (2.0 / jnp.pi) ** 0.5
    squares = values * values
    curve = jnp.tanh(scale * values * (1.0 + 0.044715 * squares))
    half = 0.5 * (1.0 + curve)
    slope = half + 0.5 * values * (1.0 - curve * curve) * (
        scale * (1.0 + 3 * 0.044715 * squares)
    )
    return values * half, slope


def dot(left, right):
    return jnp.dot(left, right, preferred_element_type=jnp.float32)


def across(left, right):
    return lax.dot_general(
        left, right, (((0,), (0,)), ((), ())), preferred_element_type=jnp.float32
    )


def against(left, right):
    return lax.dot_general(
        left, right, (((1,), (1,)), ((), ())), preferred_element_type=jnp.float32
    )


def on_device(
    inputs,
    pattern,
    rank_mask,
    up_diag,
    up_cross,
    up_left,
    up_right,
    down_diag,
    down_cross,
    down_left,
    down_right,
    cotangent,
):
    levels = up_cross.shape[0]
    rank = rank_mask.shape[0]
    feats, tokens = inputs.shape
    hid = up_diag.shape[0]
    chunks = 2
    width = tokens // chunks
    highest = lax.axis_size("feat").bit_length() - 1
    level_bits = [highest - levels + level for level in range(levels)]
    order = list(range(levels))[::-1]
    gate_values = pattern.astype(jnp.float32)
    gate_blocks = pattern.astype(jnp.bfloat16)[:, :, None]
    keep = rank_mask.astype(jnp.bfloat16)[:, None]
    spans = [(feats * level, feats * (level + 1)) for level in range(levels + 1)]
    code_rows = feats * (levels + 1)

    def swap(block, level):
        return swapped(block, "feat", level_bits[level])

    def piece(block, chunk):
        return block[:, chunk * width : (chunk + 1) * width]

    down_gated = down_cross * gate_blocks
    codes, (in_first, down_far, cot_first) = exchange(
        jnp.concatenate([across(up_right, inputs), across(down_left, cotangent)]),
        level_bits,
        [(inputs, width), (down_gated, hid), (cotangent, width)],
        1,
        0,
    )
    up_code = codes[:rank] * keep
    down_back = codes[rank:] * keep
    up_gated = up_cross * gate_blocks
    up_all = jnp.concatenate(
        [up_diag] + [up_gated[level] for level in range(levels)] + [up_left], axis=1
    )
    down_all = jnp.concatenate(
        [down_diag] + [down_far[level] for level in range(levels)] + [jnp.transpose(down_right)]
    )

    up_turned = jnp.transpose(up_all)
    down_turned = jnp.transpose(down_all)

    def gathered(near, far, code, chunk):
        return jnp.concatenate(
            [piece(near, chunk), far.reshape(levels * feats, width), piece(code, chunk)]
        )

    weights = [up_all, up_turned, down_all, down_turned]
    ins = [gathered(inputs, in_first, up_code, 0)]
    cots = [gathered(cotangent, cot_first, down_back, 0)]
    (in_second, cot_second), one = chunk_step(
        level_bits,
        [(inputs, width, width), (cotangent, width, width)],
        weights + [ins[0], cots[0]],
        feats,
        2,
    )
    ins.append(gathered(inputs, in_second, up_code, 1))
    cots.append(gathered(cotangent, cot_second, down_back, 1))
    (back_first,), two = chunk_step(
        level_bits,
        [(one[4], 0, 2 * width)],
        weights + [ins[1], cots[1], cots[0], one[0]],
        feats,
        3,
    )
    grads_down = two[6]
    grads_sent = grads_down[feats:code_rows].astype(jnp.bfloat16).reshape(levels, feats, hid)
    codes, (back_second, grad_parts, grads_up) = exchange(
        jnp.concatenate([one[5], two[5]], axis=1),
        level_bits,
        [(two[4], 2 * width), (grads_sent, hid)],
        1,
        1,
        (one[1], two[1], ins[0], ins[1]),
    )
    out_near, in_near = [one[2], two[2]], [one[3], two[3]]
    back = [back_first, back_second]
    down_code = codes[:rank] * keep
    up_back = codes[rank:] * keep

    grad_up_diag = grads_up[:, :feats]
    grad_up_cross = jnp.stack(
        [
            gate_values[level, 0] * grads_up[:, slice(*spans[level + 1])]
            for level in range(levels)
        ]
    )
    grad_up_left = grads_up[:, code_rows:]
    grad_down_diag = grads_down[:feats]
    grad_down_right = jnp.transpose(grads_down[code_rows:])
    grad_down_cross = jnp.stack(
        [gate_values[level, 0] * grad_parts[level].astype(jnp.float32) for level in range(levels)]
    )
    grad_down_left = against(cotangent, down_code)
    grad_up_right = against(inputs, up_back)

    output, input_grad = [], []
    for chunk in range(chunks):
        result = out_near[chunk] + dot(down_left, piece(down_code, chunk))
        in_grad = in_near[chunk] + dot(up_right, piece(up_back, chunk))
        for level in order[::-1]:
            result = result + back[chunk][level][:, :width].astype(jnp.float32)
            in_grad = in_grad + back[chunk][level][:, width:].astype(jnp.float32)
        output.append(result.astype(jnp.bfloat16))
        input_grad.append(in_grad.astype(jnp.bfloat16))
    output = jnp.concatenate(output, axis=1)
    input_grad = jnp.concatenate(input_grad, axis=1)
    return (
        output,
        input_grad,
        grad_up_diag,
        grad_up_cross,
        grad_up_left,
        grad_up_right,
        grad_down_diag,
        grad_down_cross,
        grad_down_left,
        grad_down_right,
    )


def solution(mesh):
    in_specs = (
        P("feat", "grp"),
        P(None, "feat"),
        P(),
        P("feat", None),
        P(None, "feat", None),
        P("feat", None),
        P("feat", None),
        P("feat", None),
        P(None, "feat", None),
        P("feat", None),
        P("feat", None),
        P("feat", "grp"),
    )
    out_specs = (
        P("feat", "grp"),
        P("feat", "grp"),
        P("feat", "grp"),
        P(None, "feat", "grp"),
        P("feat", "grp"),
        P("feat", "grp"),
        P("feat", "grp"),
        P(None, "feat", "grp"),
        P("feat", "grp"),
        P("feat", "grp"),
    )
    return jax.shard_map(
        on_device, mesh=mesh, in_specs=in_specs, out_specs=out_specs, check_vma=False
    )
```

time: 970 us -> 531 us (0.55)
  waiting for transfers between devices: 669 us -> 0 us
  Pallas kernels: 0 us -> 399 us
  matrix products: 234 us -> 6.65 us
  local copies, waits for them, and re-layouts: 8.35 us -> 76.7 us
  other arithmetic: 9.06 us -> 40.7 us
  starting transfers between devices: 24.4 us -> 0 us
  between operations: 15 us -> 1.01 us
    pallas_call x0 -> x4, Pallas kernels: none -> 399 us  [the longest x2 266 us: exchange(): pl.pallas_call(functools.partial(exchange_kernel, tuple(level_bits), size...]
    ppermute x24 -> x0, waiting for transfers between devices: 339 us -> none  [swapped(): return lax.ppermute(block, axis, route)]
    psum x2 -> x0, waiting for transfers between devices: 330 us -> none  [the longest x1 246 us: on_device(): lax.psum(across(down_right, hidden), 'feat') * keep]
    dot_general x14 -> x4, matrix products: 108 us -> 2.32 us  [dot(): return jnp.dot(left, right, preferred_element_type=jnp.float32)]
    dot_general x14 -> x2, matrix products: 64.4 us -> 0.94 us  [across(): lax.dot_general(left, right, (((0,), (0,)), ((), ())), preferred_element_...]
    dot_general x14 -> x2, matrix products: 62.4 us -> 3.38 us  [against(): lax.dot_general(left, right, (((1,), (1,)), ((), ())), preferred_element_...]
    ppermute x24 -> x0, starting transfers between devices: 24.3 us -> none  [swapped(): return lax.ppermute(block, axis, route)]
    concatenate x0 -> x4, local copies, waits for them, and re-layouts: none -> 23.2 us  [the longest x2 15.2 us: on_device(): jnp.concatenate([down_diag] + [down_far[level] for level in range(levels)...]
  transfers between devices with their start and end apart: 26 -> 0, of which waited for: 8 -> 0; matrix products, arithmetic and copies ran while one was open for 21% -> 0% of each run, Pallas kernels for 0% -> 0%
where the time goes in v1:
time: 531 us; the launch traced here: 524 us
  Pallas kernels  399 us (75%)
  local copies, waits for them, and re-layouts  76.7 us (14%)
  other arithmetic  40.7 us (8%)
  matrix products  6.65 us (1%)
    pallas_call x2, Pallas kernels, exchange(): pl.pallas_call(functools.partial(exchange_kernel, tuple(level_bits), size...  266 us
    pallas_call x2, Pallas kernels, chunk_step(): pl.pallas_call(functools.partial(chunk_kernel, tuple(level_bits), tuple((...  133 us
    unnamed x78, local copies, waits for them, and re-layouts  26.1 us
    concatenate x2, local copies, waits for them, and re-layouts, on_device(): jnp.concatenate([down_diag] + [down_far[level] for level in range(levels)...  15.2 us
    another operation x2, other arithmetic, on_device(): jnp.stack([gate_values[level, 0] * grads_up[:, slice(*spans[level + 1])]...  11.2 us

profile of v1, /device:TPU:0, one launch (start us, length us, event | category | flops | bytes accessed | tf_op | source)
XLA Modules:
  0.0 523.7 jit_solution(17165920160476883005)
XLA Ops:
  1.4 4.0 broadcast_multiply_fusion.refs_1_
  5.9 0.8 copy-done.1
  7.2 1.5 pad_maximum_fusion.6
  8.7 120.8 %shard_map.195 = (bf16[16,16,2048]{2,1,0:T(8,128)(2,1)}, bf16[4,320,1024]{2,1,0:T(8,128)(2,1)}, bf16[4,320,1280]{2,1,0:T(8,128)(2,1)}, bf16[4,320,1024]{2,1,0:T(8,128)(2,1)}) custom-call(f32[16,16,2048]{2,1,0:T(8,128)} %bitcast.151, bf16[320,2048]{1,0:T(8,128)(2,1)} %refs_0_.3, bf16[4,320,1280]{2,1,0:T(8,128)(2,1)} %broadcast_multiply_fusion.refs_1_, ...), custom_call_target="tpu_custom_call" | custom-call | tf_op jit(solution)/shard_map/pallas_call | solution.py:289
  129.6 1.3 fusion.35
  131.0 0.9 fusion.36
  132.4 0.9 fusion.32
  133.3 2.0 pad_maximum_fusion.3.refs_7_
  135.4 0.9 fusion.33
  136.3 1.0 copy-done.10
  137.3 2.0 pad_maximum_fusion.2.refs_6_.refs_4_
  139.4 1.2 copy-done.8
  140.5 3.6 copy.23
  144.1 3.8 slice_bitcast_fusion.8
  147.9 1.6 copy.27
  149.5 7.9 %concatenate.32 = bf16[1728,1280]{0,1:T(8,128)(2,1)} concatenate(bf16[320,1280]{0,1:T(8,128)(2,1)S(1)} %copy.27, bf16[320,1280]{0,1:T(8,128)(2,1)} %get-tuple-element.82, bf16[320,1280]{0,1:T(8,128)(2,1)} %get-tuple-element.81, bf16[320,1280]{0,1:T(8,128)(2,1)S(1)} %get-tuple-element.80, bf16[320,1280]{0,1:T(8,128)(2,1)S(1)} %get-tuple-element.79, bf16[128,1280]{0,1:T(8,128)(2,1)S(1)} %bitcast.159), dimensions={0} | concatenate | bytes 8847360 | tf_op jit(solution)/shard_map/concatenate | solution.py:399
  157.4 7.4 %copy.29.refs_4_.refs_3_ = bf16[1728,1280]{1,0:T(8,128)(2,1)} copy(bf16[1728,1280]{0,1:T(8,128)(2,1)} %concatenate.32) | data formatting | bytes 8847360 | tf_op jit(solution)/shard_map/concatenate | solution.py:399
  165.0 0.9 copy-done.24
  165.9 1.0 constant_dynamic-update-slice_fusion.1
  166.9 1.0 fusion.27
  167.9 0.9 fusion.26
  168.8 1.0 fusion.25
  169.8 1.0 fusion.24
  170.9 0.8 constant_dynamic-update-slice_fusion
  171.7 7.2 %copy.28.refs_2_.refs_1_ = bf16[1280,1728]{1,0:T(8,128)(2,1)} copy(bf16[1280,1728]{0,1:T(8,128)(2,1)} %constant_dynamic-update-slice_fusion) | data formatting | bytes 8847360 | tf_op jit(solution)/shard_map/concatenate | solution.py:396
  178.9 65.2 %shard_map.196 = (bf16[4,320,1024]{2,1,0:T(8,128)(2,1)}, bf16[4,320,1024]{2,1,0:T(8,128)(2,1)}, bf16[1280,1024]{1,0:T(8,128)(2,1)}, bf16[1280,1024]{1,0:T(8,128)...) custom-call(bf16[320,2048]{1,0:T(8,128)(2,1)} %refs_0_.3, ...), custom_call_target="tpu_custom_call" | custom-call | tf_op jit(solution)/shard_map/pallas_call | solution.py:141
  244.1 3.4 pad_maximum_fusion.5.refs_6_
  247.5 2.1 pad_maximum_fusion.4.refs_5_
  249.6 67.8 %shard_map.197 = (bf16[4,320,2048]{2,1,0:T(8,128)(2,1)}, bf16[1280,1024]{1,0:T(8,128)(2,1)}, bf16[1280,1024]{1,0:T(8,128)(2,1)}, f32[320,1024]{1,0:T(8,128)}, f3...) custom-call(bf16[4,320,2048]{2,1,0:T(8,128)(2,1)} %get-tuple-element.39.refs_0_, ...), custom_call_target="tpu_custom_call" | custom-call | tf_op jit(solution)/shard_map/pallas_call | solution.py:141
  317.4 5.0 slice.380
  322.4 1.5 pad_maximum_fusion.7
  324.0 144.9 %shard_map.198 = (bf16[16,16,2048]{2,1,0:T(8,128)(2,1)}, bf16[4,320,2048]{2,1,0:T(8,128)(2,1)}, bf16[4,320,1280]{2,1,0:T(8,128)(2,1)}, f32[1280,1728]{1,0:T(8,128)}) custom-call(f32[16,16,2048]{2,1,0:T(8,128)} %bitcast.152, bf16[4,320,2048]{2,1,0:T(8,128)(2,1)} %get-tuple-element.44.refs_0_, bf16[4,320,1280]{2,1,0:T(8,128)(2,1)} %bitcast.148, ...), custom_call_target="tpu_custom_call" | custom-call | tf_op jit(solution)/shard_map/pallas_call | solution.py:289
  469.5 6.2 %convert_multiply_fusion.3 = (f32[1,320,1280]{2,1,0:T(8,128)S(1)}, f32[1,320,1280]{2,1,0:T(8,128)S(1)}, f32[1,320,1280]{2,1,0:T(8,128)S(1)}, f32[1,320,1280]{2,1,0:T(8,128)S(1)}) fusion(bf16[4,320,1280]{2,1,0:T(8,128)(2,1)} %get-tuple-element.55, f32[]{:T(128)} %bitcast.35, f32[]{:T(128)} %bitcast.41, f32[]{:T(128)} %bitcast.39, f32[]{:T(128)} %bitcast.37), kind=kLoop, calls=%fused_computation.16 | loop fusion | flops 3276800 | bytes 9830416 | tf_op jit(solution)/shard_map/mul | solution.py:456
  475.7 3.1 pad_maximum_fusion.1
  478.8 6.3 %multiply_bitcast_fusion.3 = (f32[1,1280,320]{2,1,0:T(8,128)S(1)}, f32[1,1280,320]{2,1,0:T(8,128)S(1)}, f32[1,1280,320]{2,1,0:T(8,128)}, f32[1,1280,320]{2,1,0:T(8,128)}, f32[1280,320]{1,0:T(8,128)}) fusion(f32[1280,1728]{1,0:T(8,128)S(1)} %bitcast.150, f32[]{:T(128)} %bitcast.35, f32[]{:T(128)} %bitcast.41, f32[]{:T(128)} %bitcast.39, f32[]{:T(128)} %bitcast.37), kind=kLoop, calls=%fused_computation.12 | loop fusion | flops 1638400 | bytes 16384016 | tf_op jit(solution)/shard_map/stack | solution.py:446
  485.2 4.9 pad_maximum_fusion
  490.1 8.7 %copy.33 = f32[4,1280,320]{1,2,0:T(8,128)} copy(f32[4,1280,320]{2,1,0:T(8,128)} %pad_maximum_fusion) | data formatting | bytes 13107200
  499.0 3.3 slice_bitcast_fusion.7
  503.4 0.8 slice_bitcast_fusion.3
  505.3 1.1 pad_maximum_fusion.9
  509.0 1.1 pad_maximum_fusion.8
  510.2 2.9 copy.32
  513.0 2.2 convolution_bitcast_fusion.4
  515.3 1.2 convolution_bitcast_fusion.5
  516.4 2.4 slice.282
  518.8 2.7 slice.283
  521.5 1.1 slice_bitcast_fusion.16
  522.7 1.1 copy.34
  (80 shorter events, 8.4 us)
Async XLA Ops:
  0.6 4.8 copy-start
  1.4 4.0 copy-start.4
  5.4 1.3 copy-start.1
  5.4 1.3 copy-start.25
  129.5 1.3 copy-start.28
  130.9 1.5 copy-start.2
  131.0 2.3 copy-start.11
  133.3 2.0 copy-start.5
  135.4 2.0 copy-start.10
  137.3 3.2 copy-start.8
  147.9 1.6 copy-start.26
  157.4 7.4 %copy-start.9 = (bf16[4,1280,320]{1,2,0:T(8,128)(2,1)S(1)}, bf16[4,1280,320]{1,2,0:T(8,128)(2,1)}, u32[]{:S(2)}) copy-start(bf16[4,1280,320]{1,2,0:T(8,128)(2,1)} %param.16) | copy-start | bytes 9830404
  164.8 1.1 copy-start.24
  168.8 2.0 copy-start.27
  178.9 65.2 %copy-start.13 = (bf16[320,1024]{1,0:T(8,128)(2,1)S(1)}, bf16[320,1024]{1,0:T(8,128)(2,1)}, u32[]{:S(2)}) copy-start(bf16[320,1024]{1,0:T(8,128)(2,1)} %get-tuple-element.87) | copy-start | bytes 1966084
  178.9 65.2 %copy-start.20 = (bf16[128,1024]{1,0:T(8,128)(2,1)S(1)}, bf16[128,1024]{1,0:T(8,128)(2,1)}, u32[]{:S(2)}) copy-start(bf16[128,1024]{1,0:T(8,128)(2,1)} %get-tuple-element.95) | copy-start | bytes 786436
  244.1 3.4 copy-start.12
  244.1 3.4 copy-start.14
  244.1 3.4 copy-start.19
  317.4 5.1 copy-start.22
  317.4 5.0 copy-start.23
  469.5 9.3 %slice-start = ((s8[9175040]{0:T(1024)(128)(4,1)}), s8[4194304]{0:T(1024)(128)(4,1)S(1)}, s32[]{:S(2)}) async-start(s8[9175040]{0:T(1024)(128)(4,1)} %bitcast.149), calls=%async_computation | async-start | bytes 8388608
  469.5 9.3 %slice-start.1 = ((s8[9175040]{0:T(1024)(128)(4,1)}), s8[4194304]{0:T(1024)(128)(4,1)S(1)}, s32[]{:S(2)}) async-start(s8[9175040]{0:T(1024)(128)(4,1)} %bitcast.149), calls=%async_computation.1 | async-start | bytes 8388608
  475.7 3.1 slice-start.2
  490.1 8.7 %copy-start.21 = (bf16[16,16,2048]{2,1,0:T(8,128)(2,1)S(1)}, bf16[16,16,2048]{2,1,0:T(8,128)(2,1)}, u32[]{:S(2)}) copy-start(bf16[16,16,2048]{2,1,0:T(8,128)(2,1)} %get-tuple-element.48) | copy-start | bytes 3145732
  498.8 4.3 slice-start.3
  498.9 8.8 %copy-start.7 = (bf16[128,2048]{1,0:T(8,128)(2,1)}, bf16[128,2048]{1,0:T(8,128)(2,1)S(1)}, u32[]{:S(2)}) copy-start(bf16[128,2048]{1,0:T(8,128)(2,1)S(1)} %get-tuple-element.106) | copy-start | bytes 1572868
  499.0 3.3 copy-start.17
  499.0 4.5 slice-start.4
  503.4 1.3 copy-start.18
  505.3 1.8 copy-start.15
  507.1 1.3 copy-start.16
  510.2 2.9 copy-start.3
  510.2 5.1 copy-start.6

commit v2 on v1

--- a/solution.py
+++ b/solution.py
@@ -35,7 +35,15 @@
         if by_column:
             total[:, span] = value
         else:
-            total[span] = value
+            diag, cross, low, gate = total
+            feats = diag.shape[1]
+            levels = cross.shape[0]
+            diag[span] = value[:, :feats]
+            for level in range(levels):
+                cross[level, span] = (
+                    gate[level, 0] * value[:, feats * (level + 1) : feats * (level + 2)]
+                )
+            low[span] = value[:, feats * (levels + 1) :]
         return carry
 
     lax.fori_loop(0, extent // tile, step, 0)
@@ -163,14 +171,14 @@
     return found[: len(blocks)], found[len(blocks) :]
 
 
-def exchange_kernel(level_bits, sizes, early, pairs, part, *refs):
+def exchange_kernel(level_bits, sizes, early, pairs, part, gate, *refs):
     blocks = len(sizes)
     levels = len(level_bits)
     sources, refs = refs[:blocks], refs[blocks:]
     stored, refs = refs[:pairs], refs[pairs:]
     code, landing, refs = refs[0], refs[1 : blocks + 1], refs[blocks + 1 :]
     if pairs:
-        grads, refs = refs[0], refs[1:]
+        grads, refs = refs[:3] + (gate,), refs[3:]
     work, received, gathered, send, recv, far_send, far_recv = refs[:7]
     loaded = refs[7 : 7 + pairs]
     count = part.shape[0]
@@ -251,6 +259,10 @@
         copies.append(copy)
         if bit == bits - levels + top:
             launch(lambda index, level: level < top)
+            for load in loads:
+                load.wait()
+            if pairs:
+                outer(grads, loaded[: pairs // 2], loaded[pairs // 2 :], False)
         copy.wait_recv()
         work[pl.ds(keep, half)] = (
             held[pl.ds(keep, half)] + received[pl.ds(offset, half)]
@@ -269,23 +281,24 @@
         if bit == bits - levels + top:
             launch(lambda index, level: True)
     code[...] = gathered[...]
-    for copy in loads:
-        copy.wait()
-    if pairs:
-        outer(grads, loaded[: pairs // 2], loaded[pairs // 2 :], False)
     for copy in copies:
         copy.wait_send()
     for copy in started:
         copy.wait()
 
 
-def exchange(part, level_bits, blocks, early, number, stored=()):
+def exchange(part, gate, level_bits, blocks, early, number, stored=()):
     count = lax.axis_size("feat")
     bits = count.bit_length() - 1
     levels = len(level_bits)
     flat = part.reshape(count, 16, -1)
     sizes = tuple(size for _, size in blocks)
     copies = max(1, len(blocks) * levels)
+    made = []
+    if stored:
+        hid, feats = stored[0].shape[0], blocks[0][0].shape[-2]
+        rank = stored[-1].shape[0] - feats * (levels + 1)
+        made = [(hid, feats), (levels, hid, feats), (hid, rank)]
     found = pl.pallas_call(
         functools.partial(exchange_kernel, tuple(level_bits), sizes, early, len(stored)),
         out_shape=[jax.ShapeDtypeStruct(flat.shape, jnp.bfloat16)]
@@ -294,14 +307,16 @@
             for block, size in blocks
         ]
         + [
-            jax.ShapeDtypeStruct((stored[0].shape[0], stored[-1].shape[0]), jnp.float32)
-            for _ in stored[:1]
+            jax.ShapeDtypeStruct(shape, jnp.float32) for shape in made
         ],
-        in_specs=[pl.BlockSpec(memory_space=pltpu.VMEM)]
+        in_specs=[
+            pl.BlockSpec(memory_space=pltpu.VMEM),
+            pl.BlockSpec(memory_space=pltpu.SMEM),
+        ]
         + [pl.BlockSpec(memory_space=pl.ANY)] * (len(blocks) + len(stored)),
         out_specs=[pl.BlockSpec(memory_space=pltpu.VMEM)]
         + [pl.BlockSpec(memory_space=pl.ANY)] * len(blocks)
-        + [pl.BlockSpec(memory_space=pltpu.VMEM) for _ in stored[:1]],
+        + [pl.BlockSpec(memory_space=pltpu.VMEM) for _ in made],
         scratch_shapes=[
             pltpu.VMEM(flat.shape, jnp.float32),
             pltpu.VMEM(flat.shape, jnp.float32),
@@ -316,7 +331,7 @@
         compiler_params=pltpu.CompilerParams(
             collective_id=number, has_side_effects=True, vmem_limit_bytes=56 * 2**20
         ),
-    )(flat, *[block for block, _ in blocks], *stored)
+    )(flat, gate, *[block for block, _ in blocks], *stored)
     return found[0].reshape(part.shape), found[1:]
 
 
@@ -385,6 +400,7 @@
     down_gated = down_cross * gate_blocks
     codes, (in_first, down_far, cot_first) = exchange(
         jnp.concatenate([across(up_right, inputs), across(down_left, cotangent)]),
+        gate_values,
         level_bits,
         [(inputs, width), (down_gated, hid), (cotangent, width)],
         1,
@@ -429,11 +445,12 @@
     )
     grads_down = two[6]
     grads_sent = grads_down[feats:code_rows].astype(jnp.bfloat16).reshape(levels, feats, hid)
-    codes, (back_second, grad_parts, grads_up) = exchange(
+    codes, (back_second, grad_parts, grad_up_diag, grad_up_cross, grad_up_left) = exchange(
         jnp.concatenate([one[5], two[5]], axis=1),
+        gate_values,
         level_bits,
         [(two[4], 2 * width), (grads_sent, hid)],
-        1,
+        2,
         1,
         (one[1], two[1], ins[0], ins[1]),
     )
@@ -442,14 +459,6 @@
     down_code = codes[:rank] * keep
     up_back = codes[rank:] * keep
 
-    grad_up_diag = grads_up[:, :feats]
-    grad_up_cross = jnp.stack(
-        [
-            gate_values[level, 0] * grads_up[:, slice(*spans[level + 1])]
-            for level in range(levels)
-        ]
-    )
-    grad_up_left = grads_up[:, code_rows:]
     grad_down_diag = grads_down[:feats]
     grad_down_right = jnp.transpose(grads_down[code_rows:])
     grad_down_cross = jnp.stack(

time: 531 us -> 495 us (0.932); the launches traced: 524 us -> 493 us
  Pallas kernels: 399 us -> 383 us
  other arithmetic: 40.7 us -> 29.4 us
    pallas_call x2, Pallas kernels: 266 us -> 250 us  [exchange(): pl.pallas_call(functools.partial(exchange_kernel, tuple(level_bits), size...]
    another operation x2 -> x0, other arithmetic: 11.2 us -> none  [on_device(): jnp.stack([gate_values[level, 0] * grads_up[:, slice(*spans[level + 1])]...]
    unnamed x78 -> x82, local copies, waits for them, and re-layouts: 26.1 us -> 28.6 us
where the time goes in v2:
time: 495 us; the launch traced here: 493 us
  Pallas kernels  383 us (77%)
  local copies, waits for them, and re-layouts  74.4 us (15%)
  other arithmetic  29.4 us (6%)
  matrix products  5.71 us (1%)
    pallas_call x2, Pallas kernels, exchange(): pl.pallas_call(functools.partial(exchange_kernel, tuple(level_bits), size...  250 us
    pallas_call x2, Pallas kernels, chunk_step(): pl.pallas_call(functools.partial(chunk_kernel, tuple(level_bits), tuple((...  133 us
    unnamed x82, local copies, waits for them, and re-layouts  28.6 us
    concatenate x2, local copies, waits for them, and re-layouts, on_device(): jnp.concatenate([down_diag] + [down_far[level] for level in range(levels)...  15.3 us

profile of v2, /device:TPU:0, one launch (start us, length us, event | category | flops | bytes accessed | tf_op | source)
XLA Modules:
  0.0 493.3 jit_solution(2722746672245893231)
XLA Ops:
  0.7 0.8 copy.23
  2.7 4.0 broadcast_multiply_fusion.refs_1_
  7.2 0.8 copy-done.1
  8.5 1.5 pad_maximum_fusion.5
  10.0 120.9 %shard_map.195 = (bf16[16,16,2048]{2,1,0:T(8,128)(2,1)}, bf16[4,320,1024]{2,1,0:T(8,128)(2,1)}, bf16[4,320,1280]{2,1,0:T(8,128)(2,1)}, bf16[4,320,1024]{2,1,0:T(8,128)(2,1)}) custom-call(f32[16,16,2048]{2,1,0:T(8,128)} %bitcast.142, f32[4,1]{1,0:T(4,128)} %convert_element_type.87.gate, bf16[320,2048]{1,0:T(8,128)(2,1)} %refs_0_.3, ...), custom_call_target="tpu_custom_call" | custom-call | tf_op jit(solution)/shard_map/pallas_call | solution.py:302
  130.9 1.3 fusion.35
  132.4 0.9 fusion.36
  133.7 0.9 fusion.32
  134.7 2.0 pad_maximum_fusion.2.refs_7_
  136.7 0.9 fusion.33
  137.6 1.0 copy-done.9
  138.7 2.0 pad_maximum_fusion.1.refs_6_.refs_4_
  140.7 1.2 copy-done.7
  141.9 3.6 copy.24
  145.5 3.8 slice_bitcast_fusion.8
  149.2 1.6 copy.28
  150.8 7.9 %concatenate.32 = bf16[1728,1280]{0,1:T(8,128)(2,1)} concatenate(bf16[320,1280]{0,1:T(8,128)(2,1)S(1)} %copy.28, bf16[320,1280]{0,1:T(8,128)(2,1)} %get-tuple-element.81, bf16[320,1280]{0,1:T(8,128)(2,1)} %get-tuple-element.80, bf16[320,1280]{0,1:T(8,128)(2,1)S(1)} %get-tuple-element.79, bf16[320,1280]{0,1:T(8,128)(2,1)S(1)} %get-tuple-element.78, bf16[128,1280]{0,1:T(8,128)(2,1)S(1)} %bitcast.151), dimensions={0} | concatenate | bytes 8847360 | tf_op jit(solution)/shard_map/concatenate | solution.py:415
  158.7 7.4 %copy.30.refs_4_.refs_3_ = bf16[1728,1280]{1,0:T(8,128)(2,1)} copy(bf16[1728,1280]{0,1:T(8,128)(2,1)} %concatenate.32) | data formatting | bytes 8847360 | tf_op jit(solution)/shard_map/concatenate | solution.py:415
  166.4 0.9 copy-done.24
  167.2 1.0 constant_dynamic-update-slice_fusion.1
  168.2 1.0 fusion.27
  169.2 1.0 fusion.26
  170.2 1.0 fusion.25
  171.2 1.0 fusion.24
  172.3 0.7 constant_dynamic-update-slice_fusion
  173.1 7.2 %copy.29.refs_2_.refs_1_ = bf16[1280,1728]{1,0:T(8,128)(2,1)} copy(bf16[1280,1728]{0,1:T(8,128)(2,1)} %constant_dynamic-update-slice_fusion) | data formatting | bytes 8847360 | tf_op jit(solution)/shard_map/concatenate | solution.py:412
  180.3 65.1 %shard_map.196 = (bf16[4,320,1024]{2,1,0:T(8,128)(2,1)}, bf16[4,320,1024]{2,1,0:T(8,128)(2,1)}, bf16[1280,1024]{1,0:T(8,128)(2,1)}, bf16[1280,1024]{1,0:T(8,128)...) custom-call(bf16[320,2048]{1,0:T(8,128)(2,1)} %refs_0_.3, ...), custom_call_target="tpu_custom_call" | custom-call | tf_op jit(solution)/shard_map/pallas_call | solution.py:149
  245.5 3.4 pad_maximum_fusion.4.refs_6_
  248.9 2.1 pad_maximum_fusion.3.refs_5_
  251.0 67.7 %shard_map.197 = (bf16[4,320,2048]{2,1,0:T(8,128)(2,1)}, bf16[1280,1024]{1,0:T(8,128)(2,1)}, bf16[1280,1024]{1,0:T(8,128)(2,1)}, f32[320,1024]{1,0:T(8,128)}, f3...) custom-call(bf16[4,320,2048]{2,1,0:T(8,128)(2,1)} %get-tuple-element.41.refs_0_, ...), custom_call_target="tpu_custom_call" | custom-call | tf_op jit(solution)/shard_map/pallas_call | solution.py:149
  318.7 5.0 %slice.348 = bf16[1280,1280]{1,0:T(8,128)(2,1)} slice(f32[1728,1280]{1,0:T(8,128)} %get-tuple-element.47), slice={[320:1600], [0:1280]} | slice | bytes 6553600 | tf_op jit(solution)/shard_map/slice | solution.py:447
  323.8 1.5 pad_maximum_fusion.6
  325.3 129.0 %shard_map.198 = (bf16[16,16,2048]{2,1,0:T(8,128)(2,1)}, bf16[4,320,2048]{2,1,0:T(8,128)(2,1)}, bf16[4,320,1280]{2,1,0:T(8,128)(2,1)}, f32[1280,320]{1,0:T(8,128...) custom-call(f32[16,16,2048]{2,1,0:T(8,128)} %bitcast.141, f32[4,1]{1,0:T(4,128)} %convert_element_type.87.gate, ...), custom_call_target="tpu_custom_call" | custom-call | tf_op jit(solution)/shard_map/pallas_call | solution.py:302
  454.9 5.0 %convert_multiply_fusion.3 = (f32[1,320,1280]{2,1,0:T(8,128)S(1)}, f32[1,320,1280]{2,1,0:T(8,128)S(1)}, f32[1,320,1280]{2,1,0:T(8,128)S(1)}, f32[1,320,1280]{2,1,0:T(8,128)S(1)}) fusion(bf16[4,320,1280]{2,1,0:T(8,128)(2,1)} %get-tuple-element.59, f32[]{:T(128)} %bitcast.36, f32[]{:T(128)} %bitcast.39, f32[]{:T(128)} %bitcast.38, f32[]{:T(128)} %bitcast.37), kind=kLoop, calls=%fused_computation.11 | loop fusion | flops 3276800 | bytes 9830416 | tf_op jit(solution)/shard_map/mul | solution.py:465
  459.9 3.6 pad_maximum_fusion
  463.8 0.9 slice-done
  465.1 0.8 slice_bitcast_fusion.7
  467.3 0.8 slice_bitcast_fusion.3
  469.2 1.1 pad_maximum_fusion.8
  472.9 1.2 pad_maximum_fusion.7
  474.7 1.2 convolution_bitcast_fusion.4
  475.9 1.2 convolution_bitcast_fusion.5
  477.1 8.7 %copy.34 = f32[4,1280,320]{1,2,0:T(8,128)} copy(f32[4,1280,320]{2,1,0:T(8,128)} %get-tuple-element.63) | data formatting | bytes 13107200
  485.8 1.7 copy.33
  487.5 2.7 slice.251
  490.2 1.2 slice_bitcast_fusion.16
  491.4 1.1 copy.35
  492.5 0.8 copy.42
  (82 shorter events, 10.0 us)
Async XLA Ops:
  0.6 6.1 %copy-start = (bf16[320,128]{1,0:T(8,128)(2,1)S(1)}, bf16[320,128]{1,0:T(8,128)(2,1)}, u32[]{:S(2)}) copy-start(bf16[320,128]{1,0:T(8,128)(2,1)} %param.18) | copy-start | bytes 245764
  2.7 4.0 copy-start.4
  6.7 1.3 copy-start.1
  6.7 1.3 copy-start.25
  130.9 1.3 copy-start.30
  132.2 1.5 copy-start.2
  132.4 2.3 copy-start.10
  134.6 2.0 copy-start.5
  136.7 2.0 copy-start.9
  138.6 3.2 copy-start.7
  149.2 1.6 copy-start.27
  158.7 7.4 %copy-start.8 = (bf16[4,1280,320]{1,2,0:T(8,128)(2,1)S(1)}, bf16[4,1280,320]{1,2,0:T(8,128)(2,1)}, u32[]{:S(2)}) copy-start(bf16[4,1280,320]{1,2,0:T(8,128)(2,1)} %param.16) | copy-start | bytes 9830404
  166.1 1.1 copy-start.24
  170.2 2.0 copy-start.28
  180.3 65.2 %copy-start.12 = (bf16[320,1024]{1,0:T(8,128)(2,1)S(1)}, bf16[320,1024]{1,0:T(8,128)(2,1)}, u32[]{:S(2)}) copy-start(bf16[320,1024]{1,0:T(8,128)(2,1)} %get-tuple-element.86) | copy-start | bytes 1966084
  180.3 65.2 %copy-start.20 = (bf16[128,1024]{1,0:T(8,128)(2,1)S(1)}, bf16[128,1024]{1,0:T(8,128)(2,1)}, u32[]{:S(2)}) copy-start(bf16[128,1024]{1,0:T(8,128)(2,1)} %get-tuple-element.94) | copy-start | bytes 786436
  245.5 3.5 copy-start.11
  245.5 3.5 copy-start.13
  245.5 3.5 copy-start.19
  318.7 5.1 %copy-start.22 = (f32[256,1024]{1,0:T(8,128)S(1)}, f32[256,1024]{1,0:T(8,128)}, u32[]{:S(2)}) copy-start(f32[256,1024]{1,0:T(8,128)} %get-tuple-element.40) | copy-start | bytes 3145732
  318.7 5.0 %copy-start.23 = (f32[256,1024]{1,0:T(8,128)S(1)}, f32[256,1024]{1,0:T(8,128)}, u32[]{:S(2)}) copy-start(f32[256,1024]{1,0:T(8,128)} %get-tuple-element.45) | copy-start | bytes 3145732
  325.3 129.1 %copy-start.29 = (f32[4,1]{1,0:T(4,128)S(1)}, f32[4,1]{1,0:T(4,128)}, u32[]{:S(2)}) copy-start(f32[4,1]{1,0:T(4,128)} %convert_element_type.87.gate) | copy-start | bytes 52
  459.9 4.9 slice-start
  459.9 3.6 copy-start.21
  459.9 5.1 %slice-start.1 = ((s8[5242880]{0:T(1024)(128)(4,1)}), s8[1048576]{0:T(1024)(128)(4,1)S(1)}, s32[]{:S(2)}) async-start(s8[5242880]{0:T(1024)(128)(4,1)} %bitcast.143), calls=%async_computation.1 | async-start | bytes 2097152
  463.7 3.6 slice-start.2
  465.1 1.6 copy-start.17
  465.1 2.2 slice-start.3
  467.3 1.3 copy-start.18
  469.2 1.8 copy-start.15
  471.0 1.3 copy-start.16
  472.9 1.8 copy-start.3
  472.9 3.0 copy-start.6
  477.1 8.7 %copy-start.14 = (f32[1280,320]{1,0:T(8,128)S(1)}, f32[1280,320]{1,0:T(8,128)}, u32[]{:S(2)}) copy-start(f32[1280,320]{1,0:T(8,128)} %get-tuple-element.62) | copy-start | bytes 4915204
  490.2 2.3 copy-start.26
